TPU v7x, 256 devices: a whole 4x4x8 slice. The times are simulated.
256 devices in a mesh: member: 4 (over y), slab: 2 (over core), tile: 32 (over x, z).
Axes of the slice: x: 4, y: 4, z: 8, core: 2. Of those that a mesh axis runs over, the one named last changes fastest.
Arguments:
- prior: float32 [128, 262144], P('member', ('slab', 'tile')), may hold values from -6 to 6
- sensitivity: bfloat16 [512, 16, 64, 512], P(('slab', 'tile')), may hold values from -0.0625 to 0.0625
- pattern: int32 [512, 16], P(('slab', 'tile')), may hold values from -1 to 511, as said below
- ownership: int32 [512], replicated, may hold values from 0 to 511, each once
- observed: float32 [32768], P(('slab', 'tile')), may hold values from -8 to 8
- obs_noise: float32 [32768], P(('slab', 'tile')), may hold values from 0.3 to 3
- perturbation: float32 [128, 32768], P('member', ('slab', 'tile')), may hold values from -5 to 5
Outputs:
- increment: float32 [128, 262144], P('member', ('slab', 'tile'))
- weights: float32 [128, 128], replicated
Inputs may be any that keep to these rules, and one draw needn't show every extreme that they name: In each row of pattern the first c entries are distinct observation block numbers and the remaining 16 - c entries are -1, with 4 <= c <= 16; some row is full and some row has exactly 4 live entries.
All inputs are finite; a program needn't handle non-finite values.
Results may differ from a plain program's by a relative error of at most 0.0042.
Values may be sent and summed in bfloat16 or wider, within the bound.
A program may use at most 64 MiB of HBM per device.

v0:
```python
import math

import jax
import jax.numpy as jnp
from jax import lax
from jax.sharding import PartitionSpec as P


def local(prior, sensitivity, pattern, ownership, observed, obs_noise, perturbation):
    members_dev = prior.shape[0]
    members = members_dev * lax.axis_size("member")
    blocks_dev = sensitivity.shape[0]
    slot_count = sensitivity.shape[1]
    obs_block = sensitivity.shape[2]
    block_total = ownership.shape[0]
    obs_dev = observed.shape[0]
    owned_blocks = obs_dev // obs_block
    norm_scale = 1.0 / math.sqrt(members - 1)
    prior_bf = prior.astype(jnp.bfloat16)
    shaped = prior_bf.reshape(members_dev, blocks_dev, sensitivity.shape[3])
    contrib = jnp.einsum("bkop,mbp->bkmo", sensitivity, shaped, preferred_element_type=jnp.float32)
    contrib_rows = contrib.reshape(blocks_dev * slot_count, members_dev * obs_block)
    flat_pattern = pattern.reshape(blocks_dev * slot_count)
    storage_of = (
        jnp.zeros((block_total,), jnp.int32)
        .at[ownership]
        .set(jnp.arange(block_total, dtype=jnp.int32))
    )
    slot_rows = jnp.where(flat_pattern >= 0, storage_of[jnp.maximum(flat_pattern, 0)], block_total)
    local_rows = slot_rows - 0
    target = jnp.where((local_rows >= 0) & (local_rows < block_total), local_rows, block_total)
    placed = (
        jnp.zeros((block_total + 1, members_dev * obs_block), jnp.float32)
        .at[target]
        .add(contrib_rows)
    )
    summed = lax.psum(placed[:block_total], ("slab", "tile"))
    owned_rows = lax.dynamic_slice_in_dim(
        summed, lax.axis_index(("slab", "tile")) * owned_blocks, owned_blocks, 0
    )
    predicted = (
        owned_rows.reshape(owned_blocks, members_dev, obs_block)
        .transpose(1, 0, 2)
        .reshape(members_dev, obs_dev)
    )
    mean_pred = lax.psum(jnp.sum(predicted, axis=0), "member") / members
    spread = (predicted - mean_pred) * norm_scale / obs_noise
    innovation = (observed - predicted) / obs_noise + perturbation
    spread_all, innov_all = (
        lax.all_gather(spread, "member", axis=0, tiled=True),
        lax.all_gather(innovation, "member", axis=0, tiled=True),
    )
    gram_local = jnp.einsum("mo,ko->mk", spread_all, spread_all, precision=lax.Precision.HIGHEST)
    cross_local = jnp.einsum("mo,ko->mk", spread_all, innov_all, precision=lax.Precision.HIGHEST)
    misfit_local = jnp.sum(innov_all * innov_all)
    gram_matrix, cross_term, misfit = lax.psum(
        (gram_local, cross_local, misfit_local), ("slab", "tile")
    )
    damping = misfit / (4.0 * members * members)
    system = gram_matrix + damping * jnp.eye(members, dtype=jnp.float32)
    factor = jnp.linalg.cholesky(system)
    weights = jax.scipy.linalg.cho_solve((factor, True), cross_term)
    centred = ((weights - jnp.mean(weights, axis=0, keepdims=True)) * norm_scale).astype(
        jnp.bfloat16
    )
    member_start = lax.axis_index("member") * members_dev
    own_cols = lax.dynamic_slice_in_dim(centred, member_start, members_dev, 1)
    increment = lax.dot_general(
        own_cols,
        lax.all_gather(prior_bf, "member", axis=0, tiled=True),
        (((0,), (0,)), ((), ())),
        preferred_element_type=jnp.float32,
    )
    return (increment, weights)


def solution(mesh):
    return jax.shard_map(
        local,
        mesh=mesh,
        in_specs=(
            P("member", ("slab", "tile")),
            P(("slab", "tile"), None, None, None),
            P(("slab", "tile"), None),
            P(),
            P(("slab", "tile")),
            P(("slab", "tile")),
            P("member", ("slab", "tile")),
        ),
        out_specs=(P("member", ("slab", "tile")), P()),
        check_vma=False,
    )
```

profile of v0, /device:TPU:1, one launch (start us, length us, event | category | flops | bytes accessed | tf_op | source)
XLA Modules:
  0.0 477.4 jit_solution(6537073593213794000)
XLA Ops:
  8.0 0.7 broadcast_maximum_fusion
  8.7 0.7 broadcast_compare_fusion
  9.4 1.1 convert_element_type.7
  10.6 7.3 %convolution_bitcast_fusion = f32[8,16,32,64]{3,2,1,0:T(8,128)S(1)} fusion(bf16[8,16,64,512]{3,2,1,0:T(8,128)(2,1)} %param.8, bf16[32,8,512,1]{2,1,0,3:T(8,128)(2,1)S(1)} %bitcast.39), kind=kOutput, calls=%fused_computation.5 | convolution fusion | flops 268435456 | bytes 9699328 | tf_op jit(solution)/shard_map/bkop,mbp->bkmo/dot_general | solution.py:21
  18.8 2.4 scatter_custom_fusion
  21.3 1.3 gather_fusion
  22.6 4.3 scatter_custom_fusion.1
  26.9 4.7 slice.24
  31.6 197.7 %all-reduce.4.cloned.1.call-done = f32[512,2048]{1,0:T(8,128)} async-done(((f32[512,2048]{1,0:T(8,128)}), f32[512,2048]{1,0:T(8,128)}) %all-reduce.4.cloned.1.call-update) | async-done | bytes 4194320 | tf_op jit(solution)/shard_map/psum | solution.py:37
  229.3 0.8 constant_dynamic-slice_fusion
  230.5 8.4 %psum.36 = f32[512]{0:T(512)S(1)} all-reduce(f32[512]{0:T(512)S(1)} %reduce_sum.30), channel_id=1, replica_groups=mesh['member'=4,'slab'=2,'tile'=32] {'member'}, use_global_device_ids=true, to_apply=%region_4.5 | all-reduce | flops 512 | bytes 4096 | tf_op jit(solution)/shard_map/psum | solution.py:46
  239.0 10.0 %all_gather.10 = f32[128,512]{1,0:T(8,128)S(1)} all-gather(f32[32,512]{1,0:T(8,128)S(1)} %get-tuple-element.10), channel_id=1, replica_groups=mesh['member'=4,'slab'=2,'tile'=32] {'member'}, dimensions={0}, use_global_device_ids=true | all-gather | bytes 327680 | tf_op jit(solution)/shard_map/all_gather | solution.py:51
  249.0 9.4 %all_gather.9 = f32[128,512]{1,0:T(8,128)S(1)} all-gather(f32[32,512]{1,0:T(8,128)S(1)} %get-tuple-element.11), channel_id=1, replica_groups=mesh['member'=4,'slab'=2,'tile'=32] {'member'}, dimensions={0}, use_global_device_ids=true | all-gather | bytes 327680 | tf_op jit(solution)/shard_map/all_gather | solution.py:50
  258.4 1.0 fusion.21
  259.4 1.0 fusion.22
  261.6 135.2 %psum.38 = f32[]{:T(128)} all-reduce(f32[]{:T(128)} %multiply_reduce_fusion), channel_id=1, replica_groups=mesh['member'=4,'slab'=2,'tile'=32] {'slab','tile'}, use_global_device_ids=true, to_apply=%region_7.8 | all-reduce | flops 1 | bytes 8 | tf_op jit(solution)/shard_map/psum | solution.py:56
  397.4 43.2 %all-reduce.6.cloned.1.call-done = (f32[128,128]{1,0:T(8,128)}, f32[128,128]{1,0:T(8,128)}) async-done(((f32[128,128]{1,0:T(8,128)}, f32[128,128]{1,0:T(8,128)}), (f32[128,128]{1,0:T(8,128)}, f32[128,128]{1,0:T(8,128)})) %all-reduce.6.cloned.1.call-update) | async-done | bytes 131088 | tf_op jit(solution)/shard_map/psum | solution.py:56
  440.6 0.9 select_add_fusion
  441.6 0.9 fusion.8
  442.5 11.7 %cholesky.16 = f32[128,128]{1,0:T(8,128)S(1)} custom-call(f32[128,128]{1,0:T(8,128)S(1)} %fusion.8), custom_call_target="Cholesky" | custom-call | tf_op jit(solution)/shard_map/jit(cholesky)/cholesky | solution.py:61
  455.5 9.8 %custom-call.10 = f32[1,128,128]{1,2,0:T(8,128)S(1)} custom-call(f32[1,128,128]{2,1,0:T(8,128)S(1)} %fusion.3), custom_call_target="InvertDiagBlocksLowerTriangular" | custom-call | tf_op jit(solution)/shard_map/jit(_cho_solve)/triangular_solve | solution.py:62
  465.3 1.1 fusion.6
  466.8 0.7 copy.18
  467.7 2.3 fusion.11
  (40 shorter events, 4.5 us)
Async XLA Ops:
  8.0 221.3 %all-reduce.4.cloned.1.call-start = ((), (), s32[]{:S(2)}) async-start(), calls=%async_computation | async-start | bytes 8388608 | tf_op jit(solution)/shard_map/psum | solution.py:37
  10.5 7.5 %copy-start = (bf16[32,4096]{1,0:T(8,128)(2,1)}, bf16[32,4096]{1,0:T(8,128)(2,1)S(1)}, u32[]{:S(2)}) copy-start(bf16[32,4096]{1,0:T(8,128)(2,1)S(1)} %convert_element_type.7) | copy-start | bytes 786436
  10.6 8.1 %copy-start.4 = (s32[512]{0:T(512)S(1)}, s32[512]{0:T(512)}, u32[]{:S(2)}) copy-start(s32[512]{0:T(512)} %param.10) | copy-start | bytes 6148
  31.5 207.4 %copy-start.1 = (f32[32,512]{1,0:T(8,128)S(1)}, f32[32,512]{1,0:T(8,128)}, u32[]{:S(2)}) copy-start(f32[32,512]{1,0:T(8,128)} %param.13) | copy-start | bytes 196612
  31.5 207.4 %copy-start.2 = (f32[512]{0:T(512)S(1)}, f32[512]{0:T(512)}, u32[]{:S(2)}) copy-start(f32[512]{0:T(512)} %param.11) | copy-start | bytes 6148
  31.5 207.4 %copy-start.3 = (f32[512]{0:T(512)S(1)}, f32[512]{0:T(512)}, u32[]{:S(2)}) copy-start(f32[512]{0:T(512)} %param.12) | copy-start | bytes 6148
  31.6 409.1 %all-reduce.6.cloned.1.call-start = ((), (), s32[]{:S(2)}) async-start(), calls=%async_computation.2 | async-start | bytes 262144 | tf_op jit(solution)/shard_map/psum | solution.py:56
  260.4 207.2 %all-gather.2.cloned.1.call-start = ((), (), s32[]{:S(2)}) async-start(), calls=%async_computation.1 | async-start | bytes 1310720 | tf_op jit(solution)/shard_map/all_gather | solution.py:70
Sparse Core Ops, SparseCore 0:
  31.7 197.5 all-reduce.3
  260.5 180.0 all-reduce.5
Sparse Core Ops, SparseCore 1:
  263.3 31.1 all-gather.1
where the time goes:
time: 478 us; the launch traced here: 477 us
  waiting for transfers between devices  241 us (50%)
  blocking collectives  163 us (34%)
  other arithmetic  32.1 us (7%)
  between operations  16.2 us (3%)
  matrix products  13.2 us (3%)
  local copies, waits for them, and re-layouts  11.4 us (2%)
    psum x1, waiting for transfers between devices, local(): summed = lax.psum(placed[:block_total], ('slab', 'tile'))  198 us
    psum x1, blocking collectives, local(): lax.psum((gram_local, cross_local, misfit_local), ('slab', 'tile'))  135 us
    psum x1, waiting for transfers between devices, local(): lax.psum((gram_local, cross_local, misfit_local), ('slab', 'tile'))  43.2 us
    another operation x3, other arithmetic, local(): factor = jnp.linalg.cholesky(system)  12.4 us
    another operation x2, other arithmetic, local(): weights = jax.scipy.linalg.cho_solve((factor, True), cross_term)  10.5 us
    all_gather x1, blocking collectives, local(): lax.all_gather(innovation, 'member', axis=0, tiled=True)  10 us
  transfers between devices with their start and end apart: 3, of which 2 were waited for; matrix products, arithmetic and copies ran while one was open for 6% of the time, Pallas kernels for 0%

commit v1 on v0

v1 whole, which is shorter than its diff:
```python
import functools
import math

import jax
import jax.numpy as jnp
from jax import lax
from jax.experimental import pallas as pl
from jax.experimental.pallas import tpu as pltpu
from jax.sharding import PartitionSpec as P

MESH = pl.DeviceIdType.MESH
F32, BF16 = jnp.float32, jnp.bfloat16
HIGHEST = lax.Precision.HIGHEST

NY, NC, NX, NZ = 4, 2, 4, 8
MD = 32
NB, KB, OB, PB = 8, 16, 64, 512
PD = NB * PB
OD = 8 * OB
NE = NY * MD
NT = NX * NZ
NQ = 4
NORM = 1.0 / math.sqrt(NE - 1)


def rows_contract(a, b, precision=None):
    return lax.dot_general(
        a, b, (((1,), (1,)), ((), ())), precision=precision, preferred_element_type=F32
    )


def predict_kernel(
    prior_hbm, sens_hbm, pattern_ref, own_ref, obs_ref, noise_ref, pert_ref,
    sys_ref, prior_all,
    sens_v, prior_v, prior_bf, t_buf, u_buf, pat_buf, onehot, placed, x_in, x_sum, z_in,
    pred, pert_all, s_buf, d_buf, part, ab_in, c_in,
    load_sem, prior_sem, own_sem, g_send, g_recv, u_send, u_recv, x_send, x_recv, z_send, z_recv,
    y_send, y_recv, r_send, r_recv,
):
    y, c, t = lax.axis_index("member"), lax.axis_index("slab"), lax.axis_index("tile")
    x, z = lax.div(t, NZ), lax.rem(t, NZ)

    def wrap(v, n):
        return lax.rem(v, n)

    def device(dy, dc, dx, dz):
        return (wrap(y + dy, NY), wrap(c + dc, NC), wrap(x + dx, NX) * NZ + wrap(z + dz, NZ))

    def send(src, dst, send_sem, recv_sem, to):
        pltpu.make_async_remote_copy(
            src_ref=src, dst_ref=dst, send_sem=send_sem, recv_sem=recv_sem,
            device_id=to, device_id_type=MESH,
        ).start()

    def wait(ref, sem):
        pltpu.make_async_copy(ref, ref, sem).wait()

    load_prior = pltpu.make_async_copy(prior_hbm, prior_v, prior_sem)
    load_prior.start()
    loads = [
        pltpu.make_async_copy(sens_hbm.at[pl.ds(2 * i, 2)], sens_v.at[pl.ds(2 * i, 2)], load_sem.at[i])
        for i in range(NB // 2)
    ]
    for load in loads:
        load.start()

    column = [(dy, dc, dx) for dy in range(NY) for dc in range(NC) for dx in range(NX)][1:]
    barrier = pltpu.get_barrier_semaphore()
    for dy, dc, dx in column:
        pl.semaphore_signal(barrier, inc=1, device_id=device(dy, dc, dx, 0), device_id_type=MESH)
    for dz in range(1, NZ):
        pl.semaphore_signal(barrier, inc=1, device_id=device(0, 0, 0, dz), device_id_type=MESH)

    j = lax.broadcasted_iota(jnp.int32, (KB, 128), 1)
    k = lax.broadcasted_iota(jnp.int32, (KB, 128), 0)
    pick = (k == 2 * (j & 7) + ((j >> 4) & 1)).astype(F32)
    spread_rows = jnp.dot(pattern_ref[...].astype(F32), pick, precision=HIGHEST, preferred_element_type=F32)
    j = lax.broadcasted_iota(jnp.int32, (NB, 128), 1)
    b = lax.broadcasted_iota(jnp.int32, (NB, 128), 0)
    row = jnp.sum(
        jnp.where(b == 2 * (j >> 5) + ((j >> 3) & 1), spread_rows, 0.0), axis=0, keepdims=True
    )
    pat_buf[0] = jnp.broadcast_to(row, (8, 128))

    load_prior.wait()
    prior_bf[...] = prior_v[...].astype(BF16)
    low = lax.broadcasted_iota(jnp.int32, (16, 128), 1) < OB

    for i in range(NB // 2):
        loads[i].wait()
        for b in (2 * i, 2 * i + 1):
            out = rows_contract(
                prior_bf[:, b * PB : (b + 1) * PB], sens_v[b].reshape(KB * OB, PB)
            )
            for kp in range(KB // 2):
                t_buf[pl.ds((b * 8 + kp) * MD, MD), :] = out[:, kp * 128 : (kp + 1) * 128]
        for r in range(MD // 2):
            ta = t_buf[pl.ds(i * 16 * MD + r, 16, stride=MD), :]
            tb = t_buf[pl.ds(i * 16 * MD + r + 16, 16, stride=MD), :]
            lanes = pl.ds((r // 4) * 512 + (r % 2) * 256 + (r // 2 % 2) * 128, 128)
            u_buf[pl.ds(i * 32, 16), lanes] = jnp.where(low, ta, pltpu.roll(tb, OB, 1)).astype(BF16)
            u_buf[pl.ds(i * 32 + 16, 16), lanes] = jnp.where(low, pltpu.roll(ta, OB, 1), tb).astype(BF16)
        if i == 0:
            pl.semaphore_wait(barrier, len(column) + NZ - 1)
            sibling = device(0, 1, 0, 0)
            send(pat_buf.at[0], pat_buf.at[1], u_send.at[4], u_recv.at[4], sibling)
        send(u_buf.at[pl.ds(i * 32, 32)], u_buf.at[pl.ds(128 + i * 32, 32)], u_send.at[i], u_recv.at[i], sibling)
        if i == 0:
            for dy in range(1, NY):
                send(pert_ref, pert_all.at[y], g_send.at[0], g_recv.at[0], device(dy, 0, 0, 0))
            for dy in range(1, NY):
                send(prior_bf, prior_all.at[y], g_send.at[1], g_recv.at[1], device(dy, 0, 0, 0))
            keep_prior = pltpu.make_async_copy(prior_bf, prior_all.at[y], own_sem)
            keep_prior.start()
    pert_all[y] = pert_ref[...]

    wait(pat_buf.at[1], u_recv.at[4])
    for i in range(2):
        owned = own_ref[pl.ds(2 * c + i, 1), :].astype(F32)
        owned = jnp.broadcast_to(owned, (128, 128)).T
        for s in range(2):
            onehot[pl.ds(i * 128, 128), pl.ds(s * 128, 128)] = (
                (owned == pat_buf[s, 0:1, :]).astype(F32).astype(BF16)
            )
    for i in range(NB // 2):
        wait(u_buf.at[pl.ds(128 + i * 32, 32)], u_recv.at[i])

    for q in range(NQ):
        out = jnp.dot(onehot[...], u_buf[:, q * 512 : (q + 1) * 512], preferred_element_type=F32)
        out = jnp.concatenate(
            [out[:, :256].reshape(NT, 8, 256), out[:, 256:].reshape(NT, 8, 256)], axis=1
        )
        placed[q] = out.astype(BF16)
        for dx in range(1, NX):
            send(
                placed.at[q, pl.ds(wrap(x + dx, NX) * NZ, NZ)], x_in.at[q, dx - 1],
                x_send.at[q], x_recv.at[q], device(0, 0, dx, 0),
            )

    def reduce_x(q):
        wait(x_in.at[q], x_recv.at[q])
        total = placed[q, pl.ds(x * NZ, NZ)].astype(F32)
        for d in range(NX - 1):
            total += x_in[q, d].astype(F32)
        x_sum[q] = total.astype(BF16)
        for dz in range(1, NZ):
            send(
                x_sum.at[q, wrap(z + dz, NZ)], z_in.at[q, dz - 1],
                z_send.at[q], z_recv.at[q], device(0, 0, 0, dz),
            )

    def reduce_z(q):
        wait(z_in.at[q], z_recv.at[q])
        total = x_sum[q, z].astype(F32)
        for d in range(NZ - 1):
            total += z_in[q, d].astype(F32)
        first = pl.multiple_of(y * 128 + q * 32, 32)
        for n in range(4):
            h, l = n % 2, n // 2
            pred[pl.ds(first + n * 8, 8), :] = total[h * 8 : (h + 1) * 8, l * 128 : (l + 1) * 128]
        for dy in range(1, NY):
            send(
                pred.at[pl.ds(first, 32)], pred.at[pl.ds(first, 32)],
                y_send.at[q], y_recv.at[q], device(dy, 0, 0, 0),
            )

    for q in range(NQ):
        reduce_x(q)
        if q:
            reduce_z(q - 1)
    reduce_z(NQ - 1)
    wait(pert_all.at[pl.ds(0, NY - 1)], g_recv.at[0])
    for q in range(NQ):
        wait(pred.at[pl.ds(0, 96)], y_recv.at[q])

    low = lax.broadcasted_iota(jnp.int32, (NE // 2, 128), 1) < OB
    misfit = jnp.zeros((1, 1), F32)
    for n in range(OD // 128):
        even = pred[pl.ds(2 * n, NE // 2, stride=8), :]
        odd = pred[pl.ds(2 * n + 1, NE // 2, stride=8), :]
        first = jnp.where(low, even, pltpu.roll(odd, OB, 1))
        second = jnp.where(low, pltpu.roll(even, OB, 1), odd)
        pieces = []
        for w in range(NY):
            pieces += [first[w * 16 : (w + 1) * 16], second[w * 16 : (w + 1) * 16]]
        predicted = jnp.concatenate(pieces, axis=0)
        cols = pl.ds(n * 128, 128)
        noise = noise_ref[:, cols]
        mean = jnp.sum(predicted, axis=0, keepdims=True) / NE
        s_buf[:, cols] = (predicted - mean) * NORM / noise
        innovation = (obs_ref[:, cols] - predicted) / noise + pert_all[:, :, cols].reshape(NE, 128)
        d_buf[:, cols] = innovation
        misfit += jnp.sum(innovation * innovation, axis=(0, 1), keepdims=True)

    half = wrap(y, 2) * 64
    left = s_buf[pl.ds(pl.multiple_of(half, 64), 64), :]
    right = jnp.where(y < 2, s_buf[...], d_buf[...])
    quarter = rows_contract(left, right, HIGHEST)
    r_id = lax.broadcasted_iota(jnp.int32, (64, 128), 0) + half
    c_id = lax.broadcasted_iota(jnp.int32, (64, 128), 1)
    diagonal = jnp.logical_and(r_id == c_id, y < 2)
    quarter = quarter + jnp.where(diagonal, misfit / (4.0 * NE * NE), 0.0)
    part[...] = quarter.reshape(NC * NX, 8, 128)

    me = c * NX + x
    ab_in[me] = part[me]
    for dy, dc, dx in column:
        if dy == 0:
            to = wrap(c + dc, NC) * NX + wrap(x + dx, NX)
            send(part.at[to], ab_in.at[me], r_send.at[0], r_recv.at[0], device(0, dc, dx, 0))
    wait(ab_in.at[pl.ds(0, NC * NX - 1)], r_recv.at[0])
    total = ab_in[0]
    for n in range(1, NC * NX):
        total += ab_in[n]
    c_in[z] = total
    for dz in range(1, NZ):
        send(c_in.at[z], c_in.at[z], r_send.at[1], r_recv.at[1], device(0, 0, 0, dz))
    wait(c_in.at[pl.ds(0, NZ - 1)], r_recv.at[1])
    total = c_in[0]
    for n in range(1, NZ):
        total += c_in[n]
    rows = pl.ds(pl.multiple_of(y * 64 + me * 8, 8), 8)
    sys_ref[rows, :] = total
    for dy, dc, dx in column:
        send(sys_ref.at[rows], sys_ref.at[rows], r_send.at[2], r_recv.at[2], device(dy, dc, dx, 0))
    wait(sys_ref.at[pl.ds(0, 8 * len(column))], r_recv.at[2])

    wait(prior_all.at[pl.ds(0, NY - 1)], g_recv.at[1])
    keep_prior.wait()
    wait(pert_all.at[pl.ds(0, NY - 1)], g_send.at[0])
    wait(prior_all.at[pl.ds(0, NY - 1)], g_send.at[1])
    wait(pat_buf.at[1], u_send.at[4])
    for i in range(NB // 2):
        wait(u_buf.at[pl.ds(128 + i * 32, 32)], u_send.at[i])
    for q in range(NQ):
        wait(x_in.at[q], x_send.at[q])
        wait(z_in.at[q], z_send.at[q])
        wait(pred.at[pl.ds(0, 96)], y_send.at[q])
    wait(ab_in.at[pl.ds(0, NC * NX - 1)], r_send.at[0])
    wait(c_in.at[pl.ds(0, NZ - 1)], r_send.at[1])
    wait(sys_ref.at[pl.ds(0, 8 * len(column))], r_send.at[2])


def solve_kernel(sys_ref, prior_all, inc_ref, weights_ref, prior_v, x_buf, cen_buf, load_sem):
    load = pltpu.make_async_copy(prior_all, prior_v, load_sem)
    load.start()

    def mul(a, b):
        return jnp.dot(a, b, precision=HIGHEST, preferred_element_type=F32)

    system, cross = sys_ref[:NE, :], sys_ref[NE:, :]
    eye = (
        lax.broadcasted_iota(jnp.int32, (NE, NE), 0) == lax.broadcasted_iota(jnp.int32, (NE, NE), 1)
    ).astype(F32)
    bound = jnp.max(jnp.sum(jnp.abs(system), axis=0, keepdims=True), axis=1, keepdims=True)
    x_buf[...] = eye / bound

    def step(carry):
        count, _ = carry
        inverse = x_buf[...]
        residual = eye - mul(sys_ref[:NE, :], inverse)
        x_buf[...] = inverse + mul(inverse, residual)
        return count + 1, jnp.sum(residual * residual)

    lax.while_loop(lambda carry: jnp.logical_and(carry[0] < 48, carry[1] > 1e-7), step, (0, jnp.float32(1.0)))
    inverse = x_buf[...]
    weights = mul(inverse, cross)
    weights = weights + mul(inverse, cross - mul(system, weights))
    weights_ref[...] = weights
    centred = (weights - jnp.sum(weights, axis=0, keepdims=True) / NE) * NORM
    cen_buf[...] = centred.T
    y = lax.axis_index("member")
    own = cen_buf[pl.ds(pl.multiple_of(y * MD, MD), MD), :].astype(BF16)
    load.wait()
    for n in range(8):
        cols = pl.ds(n * 512, 512)
        inc_ref[:, cols] = jnp.dot(own, prior_v[:, :, cols].reshape(NE, 512), preferred_element_type=F32)


def local(prior, sensitivity, pattern, ownership, observed, obs_noise, perturbation):
    vmem, anywhere = pl.BlockSpec(memory_space=pltpu.VMEM), pl.BlockSpec(memory_space=pl.ANY)
    dma = pltpu.SemaphoreType.DMA
    system, prior_all = pl.pallas_call(
        predict_kernel,
        out_shape=(
            jax.ShapeDtypeStruct((2 * NE, NE), F32),
            jax.ShapeDtypeStruct((NY, MD, PD), BF16),
        ),
        in_specs=[anywhere, anywhere] + [vmem] * 5,
        out_specs=(vmem, anywhere),
        scratch_shapes=[
            pltpu.VMEM((NB, KB, OB, PB), BF16),
            pltpu.VMEM((MD, PD), F32),
            pltpu.VMEM((MD, PD), BF16),
            pltpu.VMEM((NB * KB // 2 * MD, 128), F32),
            pltpu.VMEM((256, 2048), BF16),
            pltpu.VMEM((2, 8, 128), F32),
            pltpu.VMEM((256, 256), BF16),
            pltpu.VMEM((NQ, NT, 16, 256), BF16),
            pltpu.VMEM((NQ, NX - 1, NZ, 16, 256), BF16),
            pltpu.VMEM((NQ, NZ, 16, 256), BF16),
            pltpu.VMEM((NQ, NZ - 1, 16, 256), BF16),
            pltpu.VMEM((NY * 128, 128), F32),
            pltpu.VMEM((NY, MD, OD), F32),
            pltpu.VMEM((NE, OD), F32),
            pltpu.VMEM((NE, OD), F32),
            pltpu.VMEM((NC * NX, 8, 128), F32),
            pltpu.VMEM((NC * NX, 8, 128), F32),
            pltpu.VMEM((NZ, 8, 128), F32),
            dma((NB // 2,)), dma, dma,
            dma((2,)), dma((2,)),
            dma((5,)), dma((5,)),
            dma((NQ,)), dma((NQ,)),
            dma((NQ,)), dma((NQ,)),
            dma((NQ,)), dma((NQ,)),
            dma((3,)), dma((3,)),
        ],
        compiler_params=pltpu.CompilerParams(
            collective_id=0, has_side_effects=True, vmem_limit_bytes=40 * 2**20
        ),
        name="predict",
    )(
        prior, sensitivity, pattern, ownership.reshape(4, 128), observed.reshape(1, OD),
        obs_noise.reshape(1, OD), perturbation,
    )
    return pl.pallas_call(
        solve_kernel,
        out_shape=(
            jax.ShapeDtypeStruct((MD, PD), F32),
            jax.ShapeDtypeStruct((NE, NE), F32),
        ),
        in_specs=[vmem, anywhere],
        out_specs=(vmem, vmem),
        scratch_shapes=[
            pltpu.VMEM((NY, MD, PD), BF16),
            pltpu.VMEM((NE, NE), F32),
            pltpu.VMEM((NE, NE), F32),
            dma,
        ],
        compiler_params=pltpu.CompilerParams(vmem_limit_bytes=24 * 2**20),
        name="solve",
    )(system, prior_all)


def solution(mesh):
    return jax.shard_map(
        local,
        mesh=mesh,
        in_specs=(
            P("member", ("slab", "tile")),
            P(("slab", "tile"), None, None, None),
            P(("slab", "tile"), None),
            P(),
            P(("slab", "tile")),
            P(("slab", "tile")),
            P("member", ("slab", "tile")),
        ),
        out_specs=(P("member", ("slab", "tile")), P()),
        check_vma=False,
    )
```

time: 478 us -> 67.4 us (0.14)
  waiting for transfers between devices: 241 us -> 0 us
  blocking collectives: 163 us -> 0 us
  Pallas kernels: 0 us -> 58.4 us
  other arithmetic: 32.1 us -> 0 us
  between operations: 16.2 us -> 0.65 us
  matrix products: 13.2 us -> 0 us
    psum x2 -> x0, waiting for transfers between devices: 241 us -> none  [the longest x1 198 us: local(): summed = lax.psum(placed[:block_total], ('slab', 'tile'))]
    psum x2 -> x0, blocking collectives: 144 us -> none  [the longest x1 135 us: local(): lax.psum((gram_local, cross_local, misfit_local), ('slab', 'tile'))]
    pallas_call x0 -> x2, Pallas kernels: none -> 58.4 us  [the longest x1 52.3 us: local(): pl.pallas_call(predict_kernel, out_shape=(jax.ShapeDtypeStruct((2 * NE, N...]
    another operation x5 -> x0, other arithmetic: 22.9 us -> none  [the longest x3 12.4 us: local(): factor = jnp.linalg.cholesky(system)]
    all_gather x2 -> x0, blocking collectives: 19.4 us -> none  [the longest x1 10 us: local(): lax.all_gather(innovation, 'member', axis=0, tiled=True)]
    dot_general x4 -> x0, matrix products: 11.7 us -> none  [the longest x1 7.34 us: local(): jnp.einsum('bkop,mbp->bkmo', sensitivity, shaped, preferred_element_type=...]
    unnamed x12 -> x14, local copies, waits for them, and re-layouts: 0.84 us -> 7.98 us
  transfers between devices with their start and end apart: 3 -> 0, of which waited for: 2 -> 0; matrix products, arithmetic and copies ran while one was open for 6% -> 0% of each run, Pallas kernels for 0% -> 0%
where the time goes in v1:
time: 67.4 us; the launch traced here: 67.1 us
  Pallas kernels  58.4 us (87%)
  local copies, waits for them, and re-layouts  7.98 us (12%)
    pallas_call x1, Pallas kernels, local(): pl.pallas_call(predict_kernel, out_shape=(jax.ShapeDtypeStruct((2 * NE, N...  52.3 us
    unnamed x14, local copies, waits for them, and re-layouts  7.98 us
    pallas_call x1, Pallas kernels, local(): pl.pallas_call(solve_kernel, out_shape=(jax.ShapeDtypeStruct((MD, PD), F3...  6.15 us

profile of v1, /device:TPU:1, one launch (start us, length us, event | category | flops | bytes accessed | tf_op | source)
XLA Modules:
  0.0 67.1 jit_solution(6654505455433402855)
XLA Ops:
  0.6 0.0 copy-start
  0.6 3.4 %copy-done = bf16[8,16,64,512]{3,2,1,0:T(8,128)(2,1)S(1)} copy-done((bf16[8,16,64,512]{3,2,1,0:T(8,128)(2,1)S(1)}, bf16[8,16,64,512]{3,2,1,0:T(8,128)(2,1)}, u32[]{:S(2)}) %copy-start) | copy-done | bytes 8388632
  4.0 0.0 copy-start.1
  4.0 1.0 %copy-done.1 = f32[32,4096]{1,0:T(8,128)S(1)} copy-done((f32[32,4096]{1,0:T(8,128)S(1)}, f32[32,4096]{1,0:T(8,128)}, u32[]{:S(2)}) %copy-start.1) | copy-done | bytes 524312
  5.1 0.0 copy-start.2
  5.1 0.8 %copy-done.2 = f32[32,512]{1,0:T(8,128)S(1)} copy-done((f32[32,512]{1,0:T(8,128)S(1)}, f32[32,512]{1,0:T(8,128)}, u32[]{:S(2)}) %copy-start.2) | copy-done | bytes 65560
  5.9 0.0 copy-start.3
  5.9 0.7 %copy-done.3 = s32[8,16]{1,0:T(8,128)S(1)} copy-done((s32[8,16]{1,0:T(8,128)S(1)}, s32[8,16]{1,0:T(8,128)}, u32[]{:S(2)}) %copy-start.3) | copy-done | bytes 536
  6.6 0.0 copy-start.4
  6.6 0.7 %copy-done.4 = s32[512]{0:T(512)S(1)} copy-done((s32[512]{0:T(512)S(1)}, s32[512]{0:T(512)}, u32[]{:S(2)}) %copy-start.4) | copy-done | bytes 2072
  7.3 0.0 copy-start.5
  7.3 0.7 %copy-done.5 = f32[512]{0:T(512)S(1)} copy-done((f32[512]{0:T(512)S(1)}, f32[512]{0:T(512)}, u32[]{:S(2)}) %copy-start.5) | copy-done | bytes 2072
  7.9 0.0 copy-start.6
  8.0 0.7 %copy-done.6 = f32[512]{0:T(512)S(1)} copy-done((f32[512]{0:T(512)S(1)}, f32[512]{0:T(512)}, u32[]{:S(2)}) %copy-start.6) | copy-done | bytes 2072
  8.6 52.3 %predict.1 = (f32[256,128]{1,0:T(8,128)S(1)}, bf16[4,32,4096]{2,1,0:T(8,128)(2,1)S(1)}) custom-call(f32[32,4096]{1,0:T(8,128)S(1)} %copy-done.1, bf16[8,16,64,512]{3,2,1,0:T(8,128)(2,1)S(1)} %copy-done, s32[8,16]{1,0:T(8,128)S(1)} %copy-done.3, s32[4,128]{1,0:T(4,128)S(1)} %bitcast.3, f32[1,512]{1,0:T(1,128)S(1)} %bitcast.4, f32[1,512]{1,0:T(1,128)S(1)} %bitcast.5, ...), custom_call_target="tpu_custom_call" | custom-call | tf_op jit(solution)/shard_map/predict/pallas_call | solution.py:283
  60.9 6.2 %solve.1 = (f32[32,4096]{1,0:T(8,128)}, f32[128,128]{1,0:T(8,128)}) custom-call(f32[256,128]{1,0:T(8,128)S(1)} %get-tuple-element.4.sys_ref, bf16[4,32,4096]{2,1,0:T(8,128)(2,1)S(1)} %get-tuple-element.5.prior_all), custom_call_target="tpu_custom_call" | custom-call | tf_op jit(solution)/shard_map/solve/pallas_call | solution.py:326
Async XLA Ops:
  0.6 3.4 %copy-start = (bf16[8,16,64,512]{3,2,1,0:T(8,128)(2,1)S(1)}, bf16[8,16,64,512]{3,2,1,0:T(8,128)(2,1)}, u32[]{:S(2)}) copy-start(bf16[8,16,64,512]{3,2,1,0:T(8,128)(2,1)} %sens_hbm.1) | copy-start | bytes 25165828
  4.0 1.0 %copy-start.1 = (f32[32,4096]{1,0:T(8,128)S(1)}, f32[32,4096]{1,0:T(8,128)}, u32[]{:S(2)}) copy-start(f32[32,4096]{1,0:T(8,128)} %prior_hbm.1) | copy-start | bytes 1572868
  5.1 0.8 %copy-start.2 = (f32[32,512]{1,0:T(8,128)S(1)}, f32[32,512]{1,0:T(8,128)}, u32[]{:S(2)}) copy-start(f32[32,512]{1,0:T(8,128)} %pert_ref.1) | copy-start | bytes 196612
  5.9 0.7 %copy-start.3 = (s32[8,16]{1,0:T(8,128)S(1)}, s32[8,16]{1,0:T(8,128)}, u32[]{:S(2)}) copy-start(s32[8,16]{1,0:T(8,128)} %pattern_ref.1) | copy-start | bytes 1540
  6.6 0.7 %copy-start.4 = (s32[512]{0:T(512)S(1)}, s32[512]{0:T(512)}, u32[]{:S(2)}) copy-start(s32[512]{0:T(512)} %param.10) | copy-start | bytes 6148
  7.3 0.7 %copy-start.5 = (f32[512]{0:T(512)S(1)}, f32[512]{0:T(512)}, u32[]{:S(2)}) copy-start(f32[512]{0:T(512)} %param.11) | copy-start | bytes 6148
  7.9 0.7 %copy-start.6 = (f32[512]{0:T(512)S(1)}, f32[512]{0:T(512)}, u32[]{:S(2)}) copy-start(f32[512]{0:T(512)} %param.12) | copy-start | bytes 6148

commit v2 on v1

v2 whole, which is shorter than its diff:
```python
import functools
import math

import jax
import jax.numpy as jnp
from jax import lax
from jax.experimental import pallas as pl
from jax.experimental.pallas import tpu as pltpu
from jax.sharding import PartitionSpec as P

MESH = pl.DeviceIdType.MESH
F32, BF16 = jnp.float32, jnp.bfloat16
HIGHEST = lax.Precision.HIGHEST

NY, NC, NX, NZ = 4, 2, 4, 8
MD = 32
NB, KB, OB, PB = 8, 16, 64, 512
PD = NB * PB
OD = 8 * OB
NE = NY * MD
NT = NX * NZ
NQ = 8
X_FIRST = ((0, 2), (2, 2), (4, 1))
Z_FIRST = ((5, 2), (7, 1))
NORM = 1.0 / math.sqrt(NE - 1)


def rows_contract(a, b, precision=None):
    return lax.dot_general(
        a, b, (((1,), (1,)), ((), ())), precision=precision, preferred_element_type=F32
    )


def predict_kernel(
    prior_hbm, sens_hbm, pattern_hbm, own_hbm, obs_hbm, noise_hbm, pert_hbm,
    sys_ref, prior_all,
    pattern_ref, own_ref, obs_ref, noise_ref, pert_ref,
    sens_v, prior_v, prior_bf, t_buf, u_buf, pat_buf, onehot, placed, x_in, x_own, z_in, z_all, first_sum,
    pred, pert_all, s_buf, d_buf, part, ab_in, c_in,
    load_sem, prior_sem, small_sem, own_sem, g_send, g_recv, u_send, u_recv, x_send, x_recv, z_send, z_recv,
    y_send, y_recv, r_send, r_recv,
):
    y, c, t = lax.axis_index("member"), lax.axis_index("slab"), lax.axis_index("tile")
    x, z = lax.div(t, NZ), lax.rem(t, NZ)

    def wrap(v, n):
        return lax.rem(v, n)

    def device(dy, dc, dx, dz):
        return (wrap(y + dy, NY), wrap(c + dc, NC), wrap(x + dx, NX) * NZ + wrap(z + dz, NZ))

    def send(src, dst, send_sem, recv_sem, to):
        pltpu.make_async_remote_copy(
            src_ref=src, dst_ref=dst, send_sem=send_sem, recv_sem=recv_sem,
            device_id=to, device_id_type=MESH,
        ).start()

    def wait(ref, sem):
        pltpu.make_async_copy(ref, ref, sem).wait()

    arrivals, ends = {}, []

    def expect(name, ref, send_sem, recv_sem):
        arrivals[name] = (ref, recv_sem)
        ends.append((ref, send_sem))

    def arrive(name):
        wait(*arrivals.pop(name))

    def finish():
        for name in list(arrivals):
            arrive(name)
        for pair in ends:
            wait(*pair)
        keep_prior.wait()

    load_prior = pltpu.make_async_copy(prior_hbm, prior_v, prior_sem)
    load_prior.start()
    loads = [
        pltpu.make_async_copy(sens_hbm.at[pl.ds(2 * i, 2)], sens_v.at[pl.ds(2 * i, 2)], load_sem.at[i])
        for i in range(NB // 2)
    ]
    small = [
        pltpu.make_async_copy(src, dst, small_sem.at[i])
        for i, (src, dst) in enumerate((
            (pattern_hbm, pattern_ref), (pert_hbm, pert_ref), (own_hbm, own_ref), (obs_hbm, obs_ref),
            (noise_hbm, noise_ref),
        ))
    ]
    small[0].start()
    for load in loads:
        load.start()
    for load in small[1:]:
        load.start()

    column = [(dy, dc, dx) for dy in range(NY) for dc in range(NC) for dx in range(NX)][1:]
    barrier = pltpu.get_barrier_semaphore()
    for dy, dc, dx in column:
        pl.semaphore_signal(barrier, inc=1, device_id=device(dy, dc, dx, 0), device_id_type=MESH)
    for dz in range(1, NZ):
        pl.semaphore_signal(barrier, inc=1, device_id=device(0, 0, 0, dz), device_id_type=MESH)

    small[0].wait()
    j = lax.broadcasted_iota(jnp.int32, (KB, 128), 1)
    k = lax.broadcasted_iota(jnp.int32, (KB, 128), 0)
    pick = (k == 2 * (j & 7) + ((j >> 4) & 1)).astype(F32)
    spread_rows = jnp.dot(pattern_ref[...].astype(F32), pick, precision=HIGHEST, preferred_element_type=F32)
    j = lax.broadcasted_iota(jnp.int32, (NB, 128), 1)
    b = lax.broadcasted_iota(jnp.int32, (NB, 128), 0)
    row = jnp.sum(
        jnp.where(b == 2 * (j >> 5) + ((j >> 3) & 1), spread_rows, 0.0), axis=0, keepdims=True
    )
    pat_buf[0] = jnp.broadcast_to(row, (8, 128))

    load_prior.wait()
    prior_bf[...] = prior_v[...].astype(BF16)
    low = lax.broadcasted_iota(jnp.int32, (16, 128), 1) < OB

    for i in range(NB // 2):
        loads[i].wait()
        for b in (2 * i, 2 * i + 1):
            out = rows_contract(
                prior_bf[:, b * PB : (b + 1) * PB], sens_v[b].reshape(KB * OB, PB)
            )
            for kp in range(KB // 2):
                t_buf[pl.ds((b * 8 + kp) * MD, MD), :] = out[:, kp * 128 : (kp + 1) * 128]
        for r in range(MD // 2):
            ta = t_buf[pl.ds(i * 16 * MD + r, 16, stride=MD), :]
            tb = t_buf[pl.ds(i * 16 * MD + r + 16, 16, stride=MD), :]
            lanes = pl.ds(r % 2 * 128, 128)
            u_buf[r // 2, pl.ds(i * 32, 16), lanes] = jnp.where(low, ta, pltpu.roll(tb, OB, 1)).astype(BF16)
            u_buf[r // 2, pl.ds(i * 32 + 16, 16), lanes] = jnp.where(low, pltpu.roll(ta, OB, 1), tb).astype(BF16)

    pl.semaphore_wait(barrier, len(column) + NZ - 1)
    sibling = device(0, 1, 0, 0)
    send(pat_buf.at[0], pat_buf.at[1], u_send.at[NQ], u_recv.at[NQ], sibling)
    expect("pattern", pat_buf.at[1], u_send.at[NQ], u_recv.at[NQ])
    for q in range(NQ):
        there = u_buf.at[q, pl.ds(128, 128)]
        send(u_buf.at[q, pl.ds(0, 128)], there, u_send.at[q], u_recv.at[q], sibling)
        expect(("u", q), there, u_send.at[q], u_recv.at[q])
    for load in small[1:]:
        load.wait()
    for dy in range(1, NY):
        send(pert_ref, pert_all.at[y], g_send.at[0], g_recv.at[0], device(dy, 0, 0, 0))
    expect("pert", pert_all.at[pl.ds(0, NY - 1)], g_send.at[0], g_recv.at[0])
    for dy in range(1, NY):
        send(prior_bf, prior_all.at[y], g_send.at[1], g_recv.at[1], device(dy, 0, 0, 0))
    expect("prior", prior_all.at[pl.ds(0, NY - 1)], g_send.at[1], g_recv.at[1])
    keep_prior = pltpu.make_async_copy(prior_bf, prior_all.at[y], own_sem)
    keep_prior.start()
    pert_all[y] = pert_ref[...]

    arrive("pattern")
    for i in range(2):
        owned = own_ref[pl.ds(2 * c + i, 1), :].astype(F32)
        owned = jnp.broadcast_to(owned, (128, 128)).T
        for s in range(2):
            onehot[pl.ds(i * 128, 128), pl.ds(s * 128, 128)] = (
                (owned == pat_buf[s, 0:1, :]).astype(F32).astype(BF16)
            )

    def place(group):
        for q in range(group[0], sum(group)):
            arrive(("u", q))
            out = jnp.dot(onehot[...], u_buf[q], preferred_element_type=F32)
            out = jnp.concatenate(
                [out[:, :128].reshape(NX, NZ, 8, 128), out[:, 128:].reshape(NX, NZ, 8, 128)], axis=2
            )
            placed[q] = out.astype(BF16)

    x_land = {g: (x_in if g in X_FIRST else x_own) for g in X_FIRST + Z_FIRST}
    z_land = {g: (z_all if g in Z_FIRST else z_in) for g in X_FIRST + Z_FIRST}

    def send_x(group):
        qs, land = pl.ds(*group), x_land[group]
        for dx in range(1, NX):
            to = wrap(x + dx, NX)
            src = placed.at[qs, to] if group in X_FIRST else first_sum.at[qs, to]
            send(src, land.at[qs, dx - 1], x_send.at[group[0]], x_recv.at[group[0]], device(0, 0, dx, 0))
        expect(("x", group), land.at[qs], x_send.at[group[0]], x_recv.at[group[0]])

    def send_z(group):
        qs, land = pl.ds(*group), z_land[group]
        for dz in range(1, NZ):
            to = wrap(z + dz, NZ)
            src = placed.at[qs, :, to] if group in Z_FIRST else first_sum.at[qs, to]
            send(src, land.at[qs, dz - 1], z_send.at[group[0]], z_recv.at[group[0]], device(0, 0, 0, dz))
        expect(("z", group), land.at[qs], z_send.at[group[0]], z_recv.at[group[0]])

    def sum_first(group):
        if group in X_FIRST:
            arrive(("x", group))
            for q in range(group[0], sum(group)):
                total = placed[q, x].astype(F32)
                for d in range(NX - 1):
                    total += x_in[q, d].astype(F32)
                first_sum[q] = total.astype(BF16)
            send_z(group)
        else:
            arrive(("z", group))
            for q in range(group[0], sum(group)):
                total = placed[q, :, z].astype(F32)
                for d in range(NZ - 1):
                    total += z_all[q, d].astype(F32)
                first_sum[q, pl.ds(0, NX)] = total.astype(BF16)
            send_x(group)

    def sum_second(group):
        if group in X_FIRST:
            arrive(("z", group))
            parts, own = [z_in.at[:, d] for d in range(NZ - 1)], z
        else:
            arrive(("x", group))
            parts, own = [x_own.at[:, d] for d in range(NX - 1)], x
        for q in range(group[0], sum(group)):
            total = first_sum[q, own].astype(F32)
            for p in parts:
                total += p[q].astype(F32)
            pred[pl.ds(pl.multiple_of(y * 128 + q * 16, 16), 16), :] = total
        rows = pl.ds(pl.multiple_of(y * 128 + group[0] * 16, 16), group[1] * 16)
        for dy in range(1, NY):
            send(pred.at[rows], pred.at[rows], y_send.at[group[0]], y_recv.at[group[0]], device(dy, 0, 0, 0))
        expect(("y", group), pred.at[pl.ds(0, 48 * group[1])], y_send.at[group[0]], y_recv.at[group[0]])

    (xa, xb, xc), (za, zb) = X_FIRST, Z_FIRST
    for group in (xa, za, xb, zb, xc):
        place(group)
        (send_x if group in X_FIRST else send_z)(group)
    sum_first(xa)
    sum_first(xb)
    sum_first(za)
    sum_first(xc)
    sum_second(xa)
    sum_first(zb)
    sum_second(za)
    sum_second(xb)
    sum_second(xc)
    sum_second(zb)
    arrive("pert")
    for group in X_FIRST + Z_FIRST:
        arrive(("y", group))

    low = lax.broadcasted_iota(jnp.int32, (NE // 2, 128), 1) < OB
    misfit = jnp.zeros((1, 1), F32)
    for n in range(OD // 128):
        even = pred[pl.ds(2 * n, NE // 2, stride=8), :]
        odd = pred[pl.ds(2 * n + 1, NE // 2, stride=8), :]
        first = jnp.where(low, even, pltpu.roll(odd, OB, 1))
        second = jnp.where(low, pltpu.roll(even, OB, 1), odd)
        pieces = []
        for w in range(NY):
            pieces += [first[w * 16 : (w + 1) * 16], second[w * 16 : (w + 1) * 16]]
        predicted = jnp.concatenate(pieces, axis=0)
        cols = pl.ds(n * 128, 128)
        noise = noise_ref[:, cols]
        mean = jnp.sum(predicted, axis=0, keepdims=True) / NE
        s_buf[:, cols] = (predicted - mean) * NORM / noise
        innovation = (obs_ref[:, cols] - predicted) / noise + pert_all[:, :, cols].reshape(NE, 128)
        d_buf[:, cols] = innovation
        misfit += jnp.sum(innovation * innovation, axis=(0, 1), keepdims=True)

    half = wrap(y, 2) * 64
    left = s_buf[pl.ds(pl.multiple_of(half, 64), 64), :]
    right = jnp.where(y < 2, s_buf[...], d_buf[...])
    quarter = rows_contract(left, right, HIGHEST)
    r_id = lax.broadcasted_iota(jnp.int32, (64, 128), 0) + half
    c_id = lax.broadcasted_iota(jnp.int32, (64, 128), 1)
    diagonal = jnp.logical_and(r_id == c_id, y < 2)
    quarter = quarter + jnp.where(diagonal, misfit / (4.0 * NE * NE), 0.0)
    part[...] = quarter.reshape(NC * NX, 8, 128)

    me = c * NX + x
    ab_in[me] = part[me]
    for dy, dc, dx in column:
        if dy == 0:
            to = wrap(c + dc, NC) * NX + wrap(x + dx, NX)
            send(part.at[to], ab_in.at[me], r_send.at[0], r_recv.at[0], device(0, dc, dx, 0))
    expect("ab", ab_in.at[pl.ds(0, NC * NX - 1)], r_send.at[0], r_recv.at[0])
    arrive("ab")
    total = ab_in[0]
    for n in range(1, NC * NX):
        total += ab_in[n]
    c_in[z] = total
    for dz in range(1, NZ):
        send(c_in.at[z], c_in.at[z], r_send.at[1], r_recv.at[1], device(0, 0, 0, dz))
    expect("c", c_in.at[pl.ds(0, NZ - 1)], r_send.at[1], r_recv.at[1])
    arrive("c")
    total = c_in[0]
    for n in range(1, NZ):
        total += c_in[n]
    rows = pl.ds(pl.multiple_of(y * 64 + me * 8, 8), 8)
    sys_ref[rows, :] = total
    for dy, dc, dx in column:
        send(sys_ref.at[rows], sys_ref.at[rows], r_send.at[2], r_recv.at[2], device(dy, dc, dx, 0))
    expect("rows", sys_ref.at[pl.ds(0, 8 * len(column))], r_send.at[2], r_recv.at[2])
    arrive("rows")

    finish()


def solve_kernel(sys_ref, prior_all, inc_ref, weights_ref, x_buf, w_buf, cen_buf):
    def mul(a, b):
        return jnp.dot(a, b, precision=HIGHEST, preferred_element_type=F32)

    def rough(a, b):
        return jnp.dot(a.astype(BF16), b.astype(BF16), preferred_element_type=F32)

    system, cross = sys_ref[:NE, :], sys_ref[NE:, :]
    eye = (
        lax.broadcasted_iota(jnp.int32, (NE, NE), 0) == lax.broadcasted_iota(jnp.int32, (NE, NE), 1)
    ).astype(F32)
    bound = jnp.max(jnp.sum(jnp.abs(system), axis=0, keepdims=True), axis=1, keepdims=True)
    start = eye / bound
    inverse = start
    for _ in range(4):
        inverse = inverse + rough(inverse, eye - rough(system, inverse))
    residual = eye - mul(system, inverse)
    x_buf[...] = inverse
    close = jnp.sum(residual * residual)

    @pl.when(jnp.logical_not(close < 0.01))
    def _():
        x_buf[...] = start

        def step(carry):
            count, _ = carry
            inverse = x_buf[...]
            residual = eye - mul(sys_ref[:NE, :], inverse)
            x_buf[...] = inverse + mul(inverse, residual)
            return count + 1, jnp.sum(residual * residual)

        lax.while_loop(
            lambda carry: jnp.logical_and(carry[0] < 64, carry[1] > 1e-7), step, (0, jnp.float32(1.0))
        )

    w_buf[...] = mul(x_buf[...], cross)
    scale = jnp.sum(cross * cross)

    def refine(carry):
        count, _ = carry
        residual = sys_ref[NE:, :] - mul(sys_ref[:NE, :], w_buf[...])
        w_buf[...] += mul(x_buf[...], residual)
        return count + 1, jnp.sum(residual * residual)

    enough = 1e-12 / jnp.minimum(close, 0.01)
    lax.while_loop(
        lambda carry: jnp.logical_and(carry[0] < 12, carry[1] > enough * scale), refine, (0, 2.0 * enough * scale)
    )
    weights = w_buf[...]
    weights_ref[...] = weights
    centred = (weights - jnp.sum(weights, axis=0, keepdims=True) / NE) * NORM
    cen_buf[...] = centred.T
    y = lax.axis_index("member")
    own = cen_buf[pl.ds(pl.multiple_of(y * MD, MD), MD), :].astype(BF16)
    for n in range(8):
        cols = pl.ds(n * 512, 512)
        inc_ref[:, cols] = jnp.dot(own, prior_all[:, :, cols].reshape(NE, 512), preferred_element_type=F32)


def local(prior, sensitivity, pattern, ownership, observed, obs_noise, perturbation):
    vmem, anywhere = pl.BlockSpec(memory_space=pltpu.VMEM), pl.BlockSpec(memory_space=pl.ANY)
    hbm = pl.BlockSpec(memory_space=pltpu.HBM)
    dma = pltpu.SemaphoreType.DMA
    operands = [
        pltpu.with_memory_space_constraint(a, pltpu.HBM)
        for a in (
            prior, sensitivity, pattern, ownership.reshape(4, 128), observed.reshape(1, OD),
            obs_noise.reshape(1, OD), perturbation,
        )
    ]
    system, prior_all = pl.pallas_call(
        predict_kernel,
        out_shape=(
            jax.ShapeDtypeStruct((2 * NE, NE), F32),
            jax.ShapeDtypeStruct((NY, MD, PD), BF16),
        ),
        in_specs=[hbm] * 7,
        out_specs=(vmem, anywhere),
        scratch_shapes=[
            pltpu.VMEM((NB, KB), jnp.int32),
            pltpu.VMEM((4, 128), jnp.int32),
            pltpu.VMEM((1, OD), F32),
            pltpu.VMEM((1, OD), F32),
            pltpu.VMEM((MD, OD), F32),
            pltpu.VMEM((NB, KB, OB, PB), BF16),
            pltpu.VMEM((MD, PD), F32),
            pltpu.VMEM((MD, PD), BF16),
            pltpu.VMEM((NB * KB // 2 * MD, 128), F32),
            pltpu.VMEM((NQ, 256, 256), BF16),
            pltpu.VMEM((2, 8, 128), F32),
            pltpu.VMEM((256, 256), BF16),
            pltpu.VMEM((NQ, NX, NZ, 16, 128), BF16),
            pltpu.VMEM((NQ, NX - 1, NZ, 16, 128), BF16),
            pltpu.VMEM((NQ, NX - 1, 16, 128), BF16),
            pltpu.VMEM((NQ, NZ - 1, 16, 128), BF16),
            pltpu.VMEM((NQ, NZ - 1, NX, 16, 128), BF16),
            pltpu.VMEM((NQ, NZ, 16, 128), BF16),
            pltpu.VMEM((NY * 128, 128), F32),
            pltpu.VMEM((NY, MD, OD), F32),
            pltpu.VMEM((NE, OD), F32),
            pltpu.VMEM((NE, OD), F32),
            pltpu.VMEM((NC * NX, 8, 128), F32),
            pltpu.VMEM((NC * NX, 8, 128), F32),
            pltpu.VMEM((NZ, 8, 128), F32),
            dma((NB // 2,)), dma, dma((5,)), dma,
            dma((2,)), dma((2,)),
            dma((NQ + 1,)), dma((NQ + 1,)),
            dma((NQ,)), dma((NQ,)),
            dma((NQ,)), dma((NQ,)),
            dma((NQ,)), dma((NQ,)),
            dma((3,)), dma((3,)),
        ],
        compiler_params=pltpu.CompilerParams(
            collective_id=0, has_side_effects=True, vmem_limit_bytes=40 * 2**20
        ),
        name="predict",
    )(*operands)
    return pl.pallas_call(
        solve_kernel,
        out_shape=(
            jax.ShapeDtypeStruct((MD, PD), F32),
            jax.ShapeDtypeStruct((NE, NE), F32),
        ),
        in_specs=[vmem, vmem],
        out_specs=(vmem, vmem),
        scratch_shapes=[
            pltpu.VMEM((NE, NE), F32),
            pltpu.VMEM((NE, NE), F32),
            pltpu.VMEM((NE, NE), F32),
        ],
        compiler_params=pltpu.CompilerParams(vmem_limit_bytes=24 * 2**20),
        name="solve",
    )(system, prior_all)


def solution(mesh):
    return jax.shard_map(
        local,
        mesh=mesh,
        in_specs=(
            P("member", ("slab", "tile")),
            P(("slab", "tile"), None, None, None),
            P(("slab", "tile"), None),
            P(),
            P(("slab", "tile")),
            P(("slab", "tile")),
            P("member", ("slab", "tile")),
        ),
        out_specs=(P("member", ("slab", "tile")), P()),
        check_vma=False,
    )
```

time: 67.4 us -> 58.7 us (0.87)
  local copies, waits for them, and re-layouts: 7.98 us -> 0 us
    unnamed x14 -> x0, local copies, waits for them, and re-layouts: 7.98 us -> none
    pallas_call x1, Pallas kernels: 52.3 us -> 50.5 us  [local(): pl.pallas_call(predict_kernel, out_shape=(jax.ShapeDtypeStruct((2 * NE, N...]
    pallas_call x1, Pallas kernels: 6.15 us -> 7.45 us  [local(): pl.pallas_call(solve_kernel, out_shape=(jax.ShapeDtypeStruct((MD, PD), F3...]
where the time goes in v2:
time: 58.7 us; the launch traced here: 58.6 us
  Pallas kernels  58 us (99%)
  between operations  0.64 us (1%)
    pallas_call x1, Pallas kernels, local(): pl.pallas_call(predict_kernel, out_shape=(jax.ShapeDtypeStruct((2 * NE, N...  50.5 us
    pallas_call x1, Pallas kernels, local(): pl.pallas_call(solve_kernel, out_shape=(jax.ShapeDtypeStruct((MD, PD), F3...  7.45 us

profile of v2, /device:TPU:1, one launch (start us, length us, event | category | flops | bytes accessed | tf_op | source)
XLA Modules:
  0.0 58.6 jit_solution(14921224305509023607)
XLA Ops:
  0.6 50.5 %predict.1 = (f32[256,128]{1,0:T(8,128)S(1)}, bf16[4,32,4096]{2,1,0:T(8,128)(2,1)S(1)}) custom-call(f32[32,4096]{1,0:T(8,128)} %prior_hbm.1, bf16[8,16,64,512]{3,2,1,0:T(8,128)(2,1)} %sens_hbm.1, s32[8,16]{1,0:T(8,128)} %pattern_hbm.1, s32[4,128]{1,0:T(4,128)} %bitcast.3, f32[1,512]{1,0:T(1,128)} %bitcast.4, f32[1,512]{1,0:T(1,128)} %bitcast.5, ...), custom_call_target="tpu_custom_call" | custom-call | tf_op jit(solution)/shard_map/predict/pallas_call | solution.py:372
  51.2 7.5 %solve.1 = (f32[32,4096]{1,0:T(8,128)}, f32[128,128]{1,0:T(8,128)}) custom-call(f32[256,128]{1,0:T(8,128)S(1)} %get-tuple-element.4.sys_ref, bf16[4,32,4096]{2,1,0:T(8,128)(2,1)S(1)} %get-tuple-element.5.prior_all), custom_call_target="tpu_custom_call" | custom-call | tf_op jit(solution)/shard_map/solve/pallas_call | solution.py:419

commit v3 on v2

--- a/solution.py
+++ b/solution.py
@@ -20,8 +20,12 @@
 NE = NY * MD
 NT = NX * NZ
 NQ = 8
-X_FIRST = ((0, 2), (2, 2), (4, 1))
-Z_FIRST = ((5, 2), (7, 1))
+X_FIRST, Z_FIRST = ((0, 1), (1, 2), (3, 2), (5, 1)), ((6, 1), (7, 1))
+PLACE = ((6, 1), (0, 1), (7, 1), (1, 2), (3, 2), (5, 1))
+SUMS = (
+    (0, (0, 1)), (0, (6, 1)), (0, (1, 2)), (0, (7, 1)), (0, (3, 2)), (0, (5, 1)),
+    (1, (0, 1)), (1, (6, 1)), (1, (1, 2)), (1, (7, 1)), (1, (3, 2)), (1, (5, 1)),
+)
 NORM = 1.0 / math.sqrt(NE - 1)
 
 
@@ -35,7 +39,7 @@
     prior_hbm, sens_hbm, pattern_hbm, own_hbm, obs_hbm, noise_hbm, pert_hbm,
     sys_ref, prior_all,
     pattern_ref, own_ref, obs_ref, noise_ref, pert_ref,
-    sens_v, prior_v, prior_bf, t_buf, u_buf, pat_buf, onehot, placed, x_in, x_own, z_in, z_all, first_sum,
+    sens_v, prior_v, prior_bf, t_buf, u_buf, pat_buf, owner, onehot, placed, x_in, x_own, z_in, z_all, first_sum,
     pred, pert_all, s_buf, d_buf, part, ab_in, c_in,
     load_sem, prior_sem, small_sem, own_sem, g_send, g_recv, u_send, u_recv, x_send, x_recv, z_send, z_recv,
     y_send, y_recv, r_send, r_recv,
@@ -58,10 +62,12 @@
     def wait(ref, sem):
         pltpu.make_async_copy(ref, ref, sem).wait()
 
+    started = set()
     arrivals, ends = {}, []
 
     def expect(name, ref, send_sem, recv_sem):
         arrivals[name] = (ref, recv_sem)
+        started.add(name)
         ends.append((ref, send_sem))
 
     def arrive(name):
@@ -72,7 +78,8 @@
             arrive(name)
         for pair in ends:
             wait(*pair)
-        keep_prior.wait()
+        if "prior" in started:
+            keep_prior.wait()
 
     load_prior = pltpu.make_async_copy(prior_hbm, prior_v, prior_sem)
     load_prior.start()
@@ -131,16 +138,24 @@
             u_buf[r // 2, pl.ds(i * 32, 16), lanes] = jnp.where(low, ta, pltpu.roll(tb, OB, 1)).astype(BF16)
             u_buf[r // 2, pl.ds(i * 32 + 16, 16), lanes] = jnp.where(low, pltpu.roll(ta, OB, 1), tb).astype(BF16)
 
+    for load in small[1:]:
+        load.wait()
+    for i in range(2):
+        owned = own_ref[pl.ds(2 * c + i, 1), :].astype(F32)
+        owned = jnp.broadcast_to(owned, (128, 128)).T
+        owner[pl.ds(i * 128, 128), :] = owned
+        onehot[pl.ds(i * 128, 128), pl.ds(0, 128)] = (owned == row).astype(F32).astype(BF16)
+    pert_all[y] = pert_ref[...]
+
     pl.semaphore_wait(barrier, len(column) + NZ - 1)
     sibling = device(0, 1, 0, 0)
     send(pat_buf.at[0], pat_buf.at[1], u_send.at[NQ], u_recv.at[NQ], sibling)
     expect("pattern", pat_buf.at[1], u_send.at[NQ], u_recv.at[NQ])
-    for q in range(NQ):
-        there = u_buf.at[q, pl.ds(128, 128)]
-        send(u_buf.at[q, pl.ds(0, 128)], there, u_send.at[q], u_recv.at[q], sibling)
-        expect(("u", q), there, u_send.at[q], u_recv.at[q])
-    for load in small[1:]:
-        load.wait()
+    for group in PLACE:
+        qs, at = pl.ds(*group), group[0]
+        there = u_buf.at[qs, pl.ds(128, 128)]
+        send(u_buf.at[qs, pl.ds(0, 128)], there, u_send.at[at], u_recv.at[at], sibling)
+        expect(("u", group), there, u_send.at[at], u_recv.at[at])
     for dy in range(1, NY):
         send(pert_ref, pert_all.at[y], g_send.at[0], g_recv.at[0], device(dy, 0, 0, 0))
     expect("pert", pert_all.at[pl.ds(0, NY - 1)], g_send.at[0], g_recv.at[0])
@@ -149,20 +164,12 @@
     expect("prior", prior_all.at[pl.ds(0, NY - 1)], g_send.at[1], g_recv.at[1])
     keep_prior = pltpu.make_async_copy(prior_bf, prior_all.at[y], own_sem)
     keep_prior.start()
-    pert_all[y] = pert_ref[...]
-
     arrive("pattern")
-    for i in range(2):
-        owned = own_ref[pl.ds(2 * c + i, 1), :].astype(F32)
-        owned = jnp.broadcast_to(owned, (128, 128)).T
-        for s in range(2):
-            onehot[pl.ds(i * 128, 128), pl.ds(s * 128, 128)] = (
-                (owned == pat_buf[s, 0:1, :]).astype(F32).astype(BF16)
-            )
+    onehot[:, pl.ds(128, 128)] = (owner[...] == pat_buf[1, 0:1, :]).astype(F32).astype(BF16)
 
     def place(group):
+        arrive(("u", group))
         for q in range(group[0], sum(group)):
-            arrive(("u", q))
             out = jnp.dot(onehot[...], u_buf[q], preferred_element_type=F32)
             out = jnp.concatenate(
                 [out[:, :128].reshape(NX, NZ, 8, 128), out[:, 128:].reshape(NX, NZ, 8, 128)], axis=2
@@ -223,20 +230,12 @@
             send(pred.at[rows], pred.at[rows], y_send.at[group[0]], y_recv.at[group[0]], device(dy, 0, 0, 0))
         expect(("y", group), pred.at[pl.ds(0, 48 * group[1])], y_send.at[group[0]], y_recv.at[group[0]])
 
-    (xa, xb, xc), (za, zb) = X_FIRST, Z_FIRST
-    for group in (xa, za, xb, zb, xc):
+    for group in PLACE:
         place(group)
         (send_x if group in X_FIRST else send_z)(group)
-    sum_first(xa)
-    sum_first(xb)
-    sum_first(za)
-    sum_first(xc)
-    sum_second(xa)
-    sum_first(zb)
-    sum_second(za)
-    sum_second(xb)
-    sum_second(xc)
-    sum_second(zb)
+
+    for stage, group in SUMS:
+        (sum_second if stage else sum_first)(group)
     arrive("pert")
     for group in X_FIRST + Z_FIRST:
         arrive(("y", group))
@@ -299,7 +298,9 @@
     finish()
 
 
-def solve_kernel(sys_ref, prior_all, inc_ref, weights_ref, x_buf, w_buf, cen_buf):
+def solve_kernel(
+    sys_ref, prior_all, inc_hbm, weights_hbm, x_buf, w_buf, cen_buf, inc_buf, out_sem
+):
     def mul(a, b):
         return jnp.dot(a, b, precision=HIGHEST, preferred_element_type=F32)
 
@@ -312,8 +313,9 @@
     ).astype(F32)
     bound = jnp.max(jnp.sum(jnp.abs(system), axis=0, keepdims=True), axis=1, keepdims=True)
     start = eye / bound
-    inverse = start
-    for _ in range(4):
+    least = jnp.sum(jnp.sum(system, axis=0, keepdims=True), axis=1, keepdims=True) / NE
+    inverse = eye * (2.0 / (bound + jnp.maximum(least, 0.0)))
+    for _ in range(3):
         inverse = inverse + rough(inverse, eye - rough(system, inverse))
     residual = eye - mul(system, inverse)
     x_buf[...] = inverse
@@ -348,14 +350,19 @@
         lambda carry: jnp.logical_and(carry[0] < 12, carry[1] > enough * scale), refine, (0, 2.0 * enough * scale)
     )
     weights = w_buf[...]
-    weights_ref[...] = weights
+    stores = [pltpu.make_async_copy(w_buf, weights_hbm, out_sem.at[4])]
+    stores[0].start()
     centred = (weights - jnp.sum(weights, axis=0, keepdims=True) / NE) * NORM
     cen_buf[...] = centred.T
     y = lax.axis_index("member")
     own = cen_buf[pl.ds(pl.multiple_of(y * MD, MD), MD), :].astype(BF16)
-    for n in range(8):
-        cols = pl.ds(n * 512, 512)
-        inc_ref[:, cols] = jnp.dot(own, prior_all[:, :, cols].reshape(NE, 512), preferred_element_type=F32)
+    for n in range(4):
+        cols = pl.ds(n * 1024, 1024)
+        inc_buf[n] = jnp.dot(own, prior_all[:, :, cols].reshape(NE, 1024), preferred_element_type=F32)
+        stores.append(pltpu.make_async_copy(inc_buf.at[n], inc_hbm.at[:, cols], out_sem.at[n]))
+        stores[-1].start()
+    for store in stores:
+        store.wait()
 
 
 def local(prior, sensitivity, pattern, ownership, observed, obs_noise, perturbation):
@@ -389,6 +396,7 @@
             pltpu.VMEM((NB * KB // 2 * MD, 128), F32),
             pltpu.VMEM((NQ, 256, 256), BF16),
             pltpu.VMEM((2, 8, 128), F32),
+            pltpu.VMEM((256, 128), F32),
             pltpu.VMEM((256, 256), BF16),
             pltpu.VMEM((NQ, NX, NZ, 16, 128), BF16),
             pltpu.VMEM((NQ, NX - 1, NZ, 16, 128), BF16),
@@ -423,11 +431,13 @@
             jax.ShapeDtypeStruct((NE, NE), F32),
         ),
         in_specs=[vmem, vmem],
-        out_specs=(vmem, vmem),
+        out_specs=(anywhere, anywhere),
         scratch_shapes=[
             pltpu.VMEM((NE, NE), F32),
             pltpu.VMEM((NE, NE), F32),
             pltpu.VMEM((NE, NE), F32),
+            pltpu.VMEM((4, MD, 1024), F32),
+            dma((5,)),
         ],
         compiler_params=pltpu.CompilerParams(vmem_limit_bytes=24 * 2**20),
         name="solve",

time: 58.7 us -> 56.4 us (0.961)
  Pallas kernels: 58 us -> 55.6 us
    pallas_call x1, Pallas kernels: 50.5 us -> 49 us  [local(): pl.pallas_call(predict_kernel, out_shape=(jax.ShapeDtypeStruct((2 * NE, N...]
    pallas_call x1, Pallas kernels: 7.45 us -> 6.66 us  [local(): pl.pallas_call(solve_kernel, out_shape=(jax.ShapeDtypeStruct((MD, PD), F3...]
where the time goes in v3:
time: 56.4 us; the launch traced here: 56.3 us
  Pallas kernels  55.6 us (99%)
  between operations  0.64 us (1%)
    pallas_call x1, Pallas kernels, local(): pl.pallas_call(predict_kernel, out_shape=(jax.ShapeDtypeStruct((2 * NE, N...  49 us
    pallas_call x1, Pallas kernels, local(): pl.pallas_call(solve_kernel, out_shape=(jax.ShapeDtypeStruct((MD, PD), F3...  6.66 us

profile of v3, /device:TPU:1, one launch (start us, length us, event | category | flops | bytes accessed | tf_op | source)
XLA Modules:
  0.0 56.3 jit_solution(11675049287350656989)
XLA Ops:
  0.6 49.0 %predict.1 = (f32[256,128]{1,0:T(8,128)S(1)}, bf16[4,32,4096]{2,1,0:T(8,128)(2,1)S(1)}) custom-call(f32[32,4096]{1,0:T(8,128)} %prior_hbm.1, bf16[8,16,64,512]{3,2,1,0:T(8,128)(2,1)} %sens_hbm.1, s32[8,16]{1,0:T(8,128)} %pattern_hbm.1, s32[4,128]{1,0:T(4,128)} %bitcast.3, f32[1,512]{1,0:T(1,128)} %bitcast.4, f32[1,512]{1,0:T(1,128)} %bitcast.5, ...), custom_call_target="tpu_custom_call" | custom-call | tf_op jit(solution)/shard_map/predict/pallas_call | solution.py:379
  49.6 6.7 %solve.1 = (f32[32,4096]{1,0:T(8,128)}, f32[128,128]{1,0:T(8,128)}) custom-call(f32[256,128]{1,0:T(8,128)S(1)} %get-tuple-element.4.sys_ref, bf16[4,32,4096]{2,1,0:T(8,128)(2,1)S(1)} %get-tuple-element.5.prior_all), custom_call_target="tpu_custom_call" | custom-call | tf_op jit(solution)/shard_map/solve/pallas_call | solution.py:427

commit v4 on v3

--- a/solution.py
+++ b/solution.py
@@ -123,20 +123,29 @@
     prior_bf[...] = prior_v[...].astype(BF16)
     low = lax.broadcasted_iota(jnp.int32, (16, 128), 1) < OB
 
-    for i in range(NB // 2):
-        loads[i].wait()
-        for b in (2 * i, 2 * i + 1):
-            out = rows_contract(
-                prior_bf[:, b * PB : (b + 1) * PB], sens_v[b].reshape(KB * OB, PB)
-            )
-            for kp in range(KB // 2):
-                t_buf[pl.ds((b * 8 + kp) * MD, MD), :] = out[:, kp * 128 : (kp + 1) * 128]
+    def slots(i):
         for r in range(MD // 2):
             ta = t_buf[pl.ds(i * 16 * MD + r, 16, stride=MD), :]
             tb = t_buf[pl.ds(i * 16 * MD + r + 16, 16, stride=MD), :]
             lanes = pl.ds(r % 2 * 128, 128)
             u_buf[r // 2, pl.ds(i * 32, 16), lanes] = jnp.where(low, ta, pltpu.roll(tb, OB, 1)).astype(BF16)
             u_buf[r // 2, pl.ds(i * 32 + 16, 16), lanes] = jnp.where(low, pltpu.roll(ta, OB, 1), tb).astype(BF16)
+
+    def product(b):
+        return rows_contract(prior_bf[:, b * PB : (b + 1) * PB], sens_v[b].reshape(KB * OB, PB))
+
+    def keep(b, out):
+        for kp in range(KB // 2):
+            t_buf[pl.ds((b * 8 + kp) * MD, MD), :] = out[:, kp * 128 : (kp + 1) * 128]
+
+    for i in range(NB // 2):
+        loads[i].wait()
+        out = product(2 * i)
+        if i:
+            slots(i - 1)
+        keep(2 * i, out)
+        keep(2 * i + 1, product(2 * i + 1))
+    slots(NB // 2 - 1)
 
     for load in small[1:]:
         load.wait()
@@ -317,11 +326,14 @@
     inverse = eye * (2.0 / (bound + jnp.maximum(least, 0.0)))
     for _ in range(3):
         inverse = inverse + rough(inverse, eye - rough(system, inverse))
-    residual = eye - mul(system, inverse)
-    x_buf[...] = inverse
-    close = jnp.sum(residual * residual)
-
-    @pl.when(jnp.logical_not(close < 0.01))
+    weights = mul(inverse, cross)
+    for _ in range(2):
+        weights = weights + mul(inverse, cross - mul(system, weights))
+    w_buf[...] = weights
+    residual = cross - mul(system, weights)
+    scale = jnp.sum(cross * cross)
+
+    @pl.when(jnp.logical_not(jnp.sum(residual * residual) <= 1e-11 * scale))
     def _():
         x_buf[...] = start
 
@@ -335,20 +347,11 @@
         lax.while_loop(
             lambda carry: jnp.logical_and(carry[0] < 64, carry[1] > 1e-7), step, (0, jnp.float32(1.0))
         )
-
-    w_buf[...] = mul(x_buf[...], cross)
-    scale = jnp.sum(cross * cross)
-
-    def refine(carry):
-        count, _ = carry
-        residual = sys_ref[NE:, :] - mul(sys_ref[:NE, :], w_buf[...])
-        w_buf[...] += mul(x_buf[...], residual)
-        return count + 1, jnp.sum(residual * residual)
-
-    enough = 1e-12 / jnp.minimum(close, 0.01)
-    lax.while_loop(
-        lambda carry: jnp.logical_and(carry[0] < 12, carry[1] > enough * scale), refine, (0, 2.0 * enough * scale)
-    )
+        w_buf[...] = mul(x_buf[...], sys_ref[NE:, :])
+        for _ in range(2):
+            residual = sys_ref[NE:, :] - mul(sys_ref[:NE, :], w_buf[...])
+            w_buf[...] += mul(x_buf[...], residual)
+
     weights = w_buf[...]
     stores = [pltpu.make_async_copy(w_buf, weights_hbm, out_sem.at[4])]
     stores[0].start()

time: 56.4 us -> 57.6 us (1.021)
  Pallas kernels: 55.6 us -> 56.9 us
    pallas_call x1, Pallas kernels: 6.66 us -> 8.15 us  [local(): pl.pallas_call(solve_kernel, out_shape=(jax.ShapeDtypeStruct((MD, PD), F3...]
where the time goes in v4:
time: 57.6 us; the launch traced here: 57.5 us
  Pallas kernels  56.9 us (99%)
  between operations  0.64 us (1%)
    pallas_call x1, Pallas kernels, local(): pl.pallas_call(predict_kernel, out_shape=(jax.ShapeDtypeStruct((2 * NE, N...  48.8 us
    pallas_call x1, Pallas kernels, local(): pl.pallas_call(solve_kernel, out_shape=(jax.ShapeDtypeStruct((MD, PD), F3...  8.15 us

profile of v4, /device:TPU:1, one launch (start us, length us, event | category | flops | bytes accessed | tf_op | source)
XLA Modules:
  0.0 57.5 jit_solution(9486148978472854001)
XLA Ops:
  0.6 48.8 %predict.1 = (f32[256,128]{1,0:T(8,128)S(1)}, bf16[4,32,4096]{2,1,0:T(8,128)(2,1)S(1)}) custom-call(f32[32,4096]{1,0:T(8,128)} %prior_hbm.1, bf16[8,16,64,512]{3,2,1,0:T(8,128)(2,1)} %sens_hbm.1, s32[8,16]{1,0:T(8,128)} %pattern_hbm.1, s32[4,128]{1,0:T(4,128)} %bitcast.3, f32[1,512]{1,0:T(1,128)} %bitcast.4, f32[1,512]{1,0:T(1,128)} %bitcast.5, ...), custom_call_target="tpu_custom_call" | custom-call | tf_op jit(solution)/shard_map/predict/pallas_call | solution.py:382
  49.4 8.1 %solve.1 = (f32[32,4096]{1,0:T(8,128)}, f32[128,128]{1,0:T(8,128)}) custom-call(f32[256,128]{1,0:T(8,128)S(1)} %get-tuple-element.4.sys_ref, bf16[4,32,4096]{2,1,0:T(8,128)(2,1)S(1)} %get-tuple-element.5.prior_all), custom_call_target="tpu_custom_call" | custom-call | tf_op jit(solution)/shard_map/solve/pallas_call | solution.py:430

commit v5 on v4

--- a/solution.py
+++ b/solution.py
@@ -20,11 +20,11 @@
 NE = NY * MD
 NT = NX * NZ
 NQ = 8
-X_FIRST, Z_FIRST = ((0, 1), (1, 2), (3, 2), (5, 1)), ((6, 1), (7, 1))
-PLACE = ((6, 1), (0, 1), (7, 1), (1, 2), (3, 2), (5, 1))
+X_FIRST, Z_FIRST = ((0, 1), (1, 2), (3, 2), (5, 1)), ((6, 2),)
+PLACE = ((0, 1), (6, 2), (1, 2), (3, 2), (5, 1))
 SUMS = (
-    (0, (0, 1)), (0, (6, 1)), (0, (1, 2)), (0, (7, 1)), (0, (3, 2)), (0, (5, 1)),
-    (1, (0, 1)), (1, (6, 1)), (1, (1, 2)), (1, (7, 1)), (1, (3, 2)), (1, (5, 1)),
+    (0, (0, 1)), (0, (1, 2)), (0, (6, 2)), (0, (3, 2)), (1, (0, 1)), (0, (5, 1)),
+    (1, (1, 2)), (1, (6, 2)), (1, (3, 2)), (1, (5, 1)),
 )
 NORM = 1.0 / math.sqrt(NE - 1)
 
@@ -326,14 +326,24 @@
     inverse = eye * (2.0 / (bound + jnp.maximum(least, 0.0)))
     for _ in range(3):
         inverse = inverse + rough(inverse, eye - rough(system, inverse))
-    weights = mul(inverse, cross)
+    weights = rough(inverse, cross)
     for _ in range(2):
-        weights = weights + mul(inverse, cross - mul(system, weights))
-    w_buf[...] = weights
+        weights = weights + rough(inverse, cross - mul(system, weights))
     residual = cross - mul(system, weights)
-    scale = jnp.sum(cross * cross)
-
-    @pl.when(jnp.logical_not(jnp.sum(residual * residual) <= 1e-11 * scale))
+    y = lax.axis_index("member")
+
+    def update(weights):
+        w_buf[...] = weights
+        centred = (weights - jnp.sum(weights, axis=0, keepdims=True) / NE) * NORM
+        cen_buf[...] = centred.T
+        own = cen_buf[pl.ds(pl.multiple_of(y * MD, MD), MD), :].astype(BF16)
+        for n in range(4):
+            cols = pl.ds(n * 1024, 1024)
+            inc_buf[n] = jnp.dot(own, prior_all[:, :, cols].reshape(NE, 1024), preferred_element_type=F32)
+
+    update(weights)
+
+    @pl.when(jnp.logical_not(jnp.sum(residual * residual) <= 1e-10 * jnp.sum(cross * cross)))
     def _():
         x_buf[...] = start
 
@@ -347,23 +357,16 @@
         lax.while_loop(
             lambda carry: jnp.logical_and(carry[0] < 64, carry[1] > 1e-7), step, (0, jnp.float32(1.0))
         )
-        w_buf[...] = mul(x_buf[...], sys_ref[NE:, :])
+        weights = mul(x_buf[...], sys_ref[NE:, :])
         for _ in range(2):
-            residual = sys_ref[NE:, :] - mul(sys_ref[:NE, :], w_buf[...])
-            w_buf[...] += mul(x_buf[...], residual)
-
-    weights = w_buf[...]
+            weights = weights + mul(x_buf[...], sys_ref[NE:, :] - mul(sys_ref[:NE, :], weights))
+        update(weights)
+
     stores = [pltpu.make_async_copy(w_buf, weights_hbm, out_sem.at[4])]
-    stores[0].start()
-    centred = (weights - jnp.sum(weights, axis=0, keepdims=True) / NE) * NORM
-    cen_buf[...] = centred.T
-    y = lax.axis_index("member")
-    own = cen_buf[pl.ds(pl.multiple_of(y * MD, MD), MD), :].astype(BF16)
     for n in range(4):
-        cols = pl.ds(n * 1024, 1024)
-        inc_buf[n] = jnp.dot(own, prior_all[:, :, cols].reshape(NE, 1024), preferred_element_type=F32)
-        stores.append(pltpu.make_async_copy(inc_buf.at[n], inc_hbm.at[:, cols], out_sem.at[n]))
-        stores[-1].start()
+        stores.append(pltpu.make_async_copy(inc_buf.at[n], inc_hbm.at[:, pl.ds(n * 1024, 1024)], out_sem.at[n]))
+    for store in stores:
+        store.start()
     for store in stores:
         store.wait()
 

time: 57.6 us -> 58.1 us (level)
  no operation moved by 1% of the time
where the time goes in v5:
time: 58.1 us; the launch traced here: 58 us
  Pallas kernels  57.4 us (99%)
  between operations  0.64 us (1%)
    pallas_call x1, Pallas kernels, local(): pl.pallas_call(predict_kernel, out_shape=(jax.ShapeDtypeStruct((2 * NE, N...  48.8 us
    pallas_call x1, Pallas kernels, local(): pl.pallas_call(solve_kernel, out_shape=(jax.ShapeDtypeStruct((MD, PD), F3...  8.61 us

profile of v5, /device:TPU:1, one launch (start us, length us, event | category | flops | bytes accessed | tf_op | source)
XLA Modules:
  0.0 58.0 jit_solution(9018816317172851598)
XLA Ops:
  0.6 48.8 %predict.1 = (f32[256,128]{1,0:T(8,128)S(1)}, bf16[4,32,4096]{2,1,0:T(8,128)(2,1)S(1)}) custom-call(f32[32,4096]{1,0:T(8,128)} %prior_hbm.1, bf16[8,16,64,512]{3,2,1,0:T(8,128)(2,1)} %sens_hbm.1, s32[8,16]{1,0:T(8,128)} %pattern_hbm.1, s32[4,128]{1,0:T(4,128)} %bitcast.3, f32[1,512]{1,0:T(1,128)} %bitcast.4, f32[1,512]{1,0:T(1,128)} %bitcast.5, ...), custom_call_target="tpu_custom_call" | custom-call | tf_op jit(solution)/shard_map/predict/pallas_call | solution.py:385
  49.4 8.6 %solve.1 = (f32[32,4096]{1,0:T(8,128)}, f32[128,128]{1,0:T(8,128)}) custom-call(f32[256,128]{1,0:T(8,128)S(1)} %get-tuple-element.4.sys_ref, bf16[4,32,4096]{2,1,0:T(8,128)(2,1)S(1)} %get-tuple-element.5.prior_all), custom_call_target="tpu_custom_call" | custom-call | tf_op jit(solution)/shard_map/solve/pallas_call | solution.py:433

commit v6 on v5

--- a/solution.py
+++ b/solution.py
@@ -76,8 +76,8 @@
     def finish():
         for name in list(arrivals):
             arrive(name)
-        for pair in ends:
-            wait(*pair)
+        while ends:
+            wait(*ends.pop())
         if "prior" in started:
             keep_prior.wait()
 
@@ -301,10 +301,10 @@
     sys_ref[rows, :] = total
     for dy, dc, dx in column:
         send(sys_ref.at[rows], sys_ref.at[rows], r_send.at[2], r_recv.at[2], device(dy, dc, dx, 0))
+    finish()
     expect("rows", sys_ref.at[pl.ds(0, 8 * len(column))], r_send.at[2], r_recv.at[2])
     arrive("rows")
-
-    finish()
+    wait(*ends.pop())
 
 
 def solve_kernel(
@@ -320,11 +320,9 @@
     eye = (
         lax.broadcasted_iota(jnp.int32, (NE, NE), 0) == lax.broadcasted_iota(jnp.int32, (NE, NE), 1)
     ).astype(F32)
-    bound = jnp.max(jnp.sum(jnp.abs(system), axis=0, keepdims=True), axis=1, keepdims=True)
-    start = eye / bound
-    least = jnp.sum(jnp.sum(system, axis=0, keepdims=True), axis=1, keepdims=True) / NE
-    inverse = eye * (2.0 / (bound + jnp.maximum(least, 0.0)))
-    for _ in range(3):
+    size = jnp.sum(jnp.abs(system), axis=0, keepdims=True)
+    inverse = eye * (2.0 / (size + jnp.maximum(jnp.sum(system, axis=0, keepdims=True), 0.0)))
+    for _ in range(2):
         inverse = inverse + rough(inverse, eye - rough(system, inverse))
     weights = rough(inverse, cross)
     for _ in range(2):
@@ -345,7 +343,7 @@
 
     @pl.when(jnp.logical_not(jnp.sum(residual * residual) <= 1e-10 * jnp.sum(cross * cross)))
     def _():
-        x_buf[...] = start
+        x_buf[...] = eye / jnp.max(size, axis=1, keepdims=True)
 
         def step(carry):
             count, _ = carry

time: 58.1 us -> 57.6 us (level)
  Pallas kernels: 57.4 us -> 56.6 us
    pallas_call x1, Pallas kernels: 8.61 us -> 7.89 us  [local(): pl.pallas_call(solve_kernel, out_shape=(jax.ShapeDtypeStruct((MD, PD), F3...]
where the time goes in v6:
time: 57.6 us; the launch traced here: 57.3 us
  Pallas kernels  56.6 us (98%)
  between operations  0.64 us (1%)
    pallas_call x1, Pallas kernels, local(): pl.pallas_call(predict_kernel, out_shape=(jax.ShapeDtypeStruct((2 * NE, N...  48.7 us
    pallas_call x1, Pallas kernels, local(): pl.pallas_call(solve_kernel, out_shape=(jax.ShapeDtypeStruct((MD, PD), F3...  7.89 us

profile of v6, /device:TPU:1, one launch (start us, length us, event | category | flops | bytes accessed | tf_op | source)
XLA Modules:
  0.0 57.3 jit_solution(16807772742781413321)
XLA Ops:
  0.6 48.7 %predict.1 = (f32[256,128]{1,0:T(8,128)S(1)}, bf16[4,32,4096]{2,1,0:T(8,128)(2,1)S(1)}) custom-call(f32[32,4096]{1,0:T(8,128)} %prior_hbm.1, bf16[8,16,64,512]{3,2,1,0:T(8,128)(2,1)} %sens_hbm.1, s32[8,16]{1,0:T(8,128)} %pattern_hbm.1, s32[4,128]{1,0:T(4,128)} %bitcast.3, f32[1,512]{1,0:T(1,128)} %bitcast.4, f32[1,512]{1,0:T(1,128)} %bitcast.5, ...), custom_call_target="tpu_custom_call" | custom-call | tf_op jit(solution)/shard_map/predict/pallas_call | solution.py:383
  49.4 7.9 %solve.1 = (f32[32,4096]{1,0:T(8,128)}, f32[128,128]{1,0:T(8,128)}) custom-call(f32[256,128]{1,0:T(8,128)S(1)} %get-tuple-element.4.sys_ref, bf16[4,32,4096]{2,1,0:T(8,128)(2,1)S(1)} %get-tuple-element.5.prior_all), custom_call_target="tpu_custom_call" | custom-call | tf_op jit(solution)/shard_map/solve/pallas_call | solution.py:431

commit v7 on v6

--- a/solution.py
+++ b/solution.py
@@ -329,20 +329,27 @@
         weights = weights + rough(inverse, cross - mul(system, weights))
     residual = cross - mul(system, weights)
     y = lax.axis_index("member")
+    stores = [pltpu.make_async_copy(w_buf, weights_hbm, out_sem.at[4])]
+    for n in range(4):
+        stores.append(pltpu.make_async_copy(inc_buf.at[n], inc_hbm.at[:, pl.ds(n * 1024, 1024)], out_sem.at[n]))
 
     def update(weights):
         w_buf[...] = weights
+        stores[0].start()
         centred = (weights - jnp.sum(weights, axis=0, keepdims=True) / NE) * NORM
         cen_buf[...] = centred.T
         own = cen_buf[pl.ds(pl.multiple_of(y * MD, MD), MD), :].astype(BF16)
         for n in range(4):
             cols = pl.ds(n * 1024, 1024)
             inc_buf[n] = jnp.dot(own, prior_all[:, :, cols].reshape(NE, 1024), preferred_element_type=F32)
+            stores[n + 1].start()
 
     update(weights)
 
     @pl.when(jnp.logical_not(jnp.sum(residual * residual) <= 1e-10 * jnp.sum(cross * cross)))
     def _():
+        for store in stores:
+            store.wait()
         x_buf[...] = eye / jnp.max(size, axis=1, keepdims=True)
 
         def step(carry):
@@ -360,11 +367,6 @@
             weights = weights + mul(x_buf[...], sys_ref[NE:, :] - mul(sys_ref[:NE, :], weights))
         update(weights)
 
-    stores = [pltpu.make_async_copy(w_buf, weights_hbm, out_sem.at[4])]
-    for n in range(4):
-        stores.append(pltpu.make_async_copy(inc_buf.at[n], inc_hbm.at[:, pl.ds(n * 1024, 1024)], out_sem.at[n]))
-    for store in stores:
-        store.start()
     for store in stores:
         store.wait()
 

time: 57.6 us -> 58.3 us (1.012)
  Pallas kernels: 56.6 us -> 57.6 us
    pallas_call x1, Pallas kernels: 7.89 us -> 8.85 us  [local(): pl.pallas_call(solve_kernel, out_shape=(jax.ShapeDtypeStruct((MD, PD), F3...]
where the time goes in v7:
time: 58.3 us; the launch traced here: 58.2 us
  Pallas kernels  57.6 us (99%)
  between operations  0.64 us (1%)
    pallas_call x1, Pallas kernels, local(): pl.pallas_call(predict_kernel, out_shape=(jax.ShapeDtypeStruct((2 * NE, N...  48.7 us
    pallas_call x1, Pallas kernels, local(): pl.pallas_call(solve_kernel, out_shape=(jax.ShapeDtypeStruct((MD, PD), F3...  8.85 us

profile of v7, /device:TPU:1, one launch (start us, length us, event | category | flops | bytes accessed | tf_op | source)
XLA Modules:
  0.0 58.2 jit_solution(18444624501269258576)
XLA Ops:
  0.6 48.7 %predict.1 = (f32[256,128]{1,0:T(8,128)S(1)}, bf16[4,32,4096]{2,1,0:T(8,128)(2,1)S(1)}) custom-call(f32[32,4096]{1,0:T(8,128)} %prior_hbm.1, bf16[8,16,64,512]{3,2,1,0:T(8,128)(2,1)} %sens_hbm.1, s32[8,16]{1,0:T(8,128)} %pattern_hbm.1, s32[4,128]{1,0:T(4,128)} %bitcast.3, f32[1,512]{1,0:T(1,128)} %bitcast.4, f32[1,512]{1,0:T(1,128)} %bitcast.5, ...), custom_call_target="tpu_custom_call" | custom-call | tf_op jit(solution)/shard_map/predict/pallas_call | solution.py:385
  49.4 8.8 %solve.1 = (f32[32,4096]{1,0:T(8,128)}, f32[128,128]{1,0:T(8,128)}) custom-call(f32[256,128]{1,0:T(8,128)S(1)} %get-tuple-element.4.sys_ref, bf16[4,32,4096]{2,1,0:T(8,128)(2,1)S(1)} %get-tuple-element.5.prior_all), custom_call_target="tpu_custom_call" | custom-call | tf_op jit(solution)/shard_map/solve/pallas_call | solution.py:433
